TPU v7x, 32 devices: a whole 2x2x4 slice. The times are simulated.
32 devices in a mesh: parts: 2 (over x), gx: 8 (over z, y), gz: 2 (over core).
Axes of the slice: x: 2, y: 2, z: 4, core: 2. Of those that a mesh axis runs over, the one named last changes fastest.
Arguments:
- velocity: float32 [3, 128, 256, 256], P(None, 'gx', 'parts', 'gz'), parts along dimension 2, may hold values from -3 to 3
- turbulence: float32 [128, 256, 256], P('gx', 'parts', 'gz'), parts along dimension 1, may hold values from 0.05 to 1
- wall_distance: float32 [128, 256, 256], P('gx', 'parts', 'gz'), parts along dimension 1, may hold values from 0.5 to 4
- porosity: float32 [128, 256, 256], P('gx', 'parts', 'gz'), parts along dimension 1, may hold values from 0.1 to 2
- solid_mask: int32 [128, 256, 256], P('gx', 'parts', 'gz'), parts along dimension 1, may hold values 0 or 1
- adj_velocity: float32 [3, 128, 256, 256], P(None, 'gx', 'parts', 'gz'), parts along dimension 2, may hold values from -6 to 6
- adj_pressure: float32 [128, 256, 256], P('gx', 'parts', 'gz'), parts along dimension 1, may hold values from -6 to 6
- adj_turbulence: float32 [128, 256, 256], P('gx', 'parts', 'gz'), parts along dimension 1, may hold values from -6 to 6
- adj_distance: float32 [128, 256, 256], P('gx', 'parts', 'gz'), parts along dimension 1, may hold values from -6 to 6
Outputs:
- new_velocity: float32 [3, 128, 256, 256], P(None, 'gx', 'parts', 'gz'), parts along dimension 2
- new_pressure: float32 [128, 256, 256], P('gx', 'parts', 'gz'), parts along dimension 1
- new_turbulence: float32 [128, 256, 256], P('gx', 'parts', 'gz'), parts along dimension 1
- new_distance: float32 [128, 256, 256], P('gx', 'parts', 'gz'), parts along dimension 1
- sensitivity: float32 [128, 256, 256], P('gx', 'parts', 'gz'), parts along dimension 1
- norms: float32 [16], P('parts'), parts along dimension 0
There are 2 independent parts, one for each index of `parts`. A program takes and returns all parts, laid end to end along the dimension named above; each array names one. Nothing has to cross between parts.
Inputs may be any that keep to these rules, and one draw needn't show every extreme that they name: `solid_mask`: 1 marks a solid cell, 0 a fluid cell.
All inputs are finite; a program needn't handle non-finite values. No bound on the sum of `solid_mask` on one device may be relied on, other than what follows from the above.
Results may differ from a plain program's by a relative error of at most 0.0001.
Values sent between devices are 32-bit elements; how exact they have to be, the bound alone decides.
A program may use at most 128 MiB of HBM per device.

v0:
```python
import functools

import jax
import jax.numpy as jnp
from jax import lax
from jax.experimental import pallas as pl
from jax.experimental.pallas import tpu as pltpu
from jax.sharding import PartitionSpec as P

VISCOSITY = 0.5
COUPLING = 0.6
DESTRUCTION = 0.3
DISTANCE_DAMPING = 0.5
PENALTY = 20.0
PAD = 8
ROWS = 8
MESH = pl.DeviceIdType.MESH


def kernel(
    ngx,
    ngz,
    velocity,
    turbulence,
    wall_distance,
    porosity,
    solid_mask,
    adj_velocity,
    adj_pressure,
    adj_turbulence,
    adj_distance,
    new_velocity,
    new_pressure,
    new_turbulence,
    new_distance,
    sensitivity,
    norms,
    first,
    second,
    flow,
    turb,
    wall,
    poros,
    solid,
    coefs,
    edge_send,
    edge_recv,
    sums,
    all_sums,
    load_sem,
    face_send_sem,
    face_recv_sem,
    edge_send_sem,
    edge_recv_sem,
    sum_send_sem,
    sum_recv_sem,
):
    nx, ny, nz = turbulence.shape
    gx = lax.axis_index("gx")
    gz = lax.axis_index("gz")
    me = gx * ngz + gz
    group = ngx * ngz
    has_low = gx > 0
    has_high = gx < ngx - 1
    body = pl.ds(PAD, ny)
    chunks = ny // ROWS

    loads = [
        pltpu.make_async_copy(adj_velocity, first.at[0:3, 1 : nx + 1, body], load_sem.at[0]),
        pltpu.make_async_copy(adj_pressure, first.at[3, 1 : nx + 1, body], load_sem.at[1]),
        pltpu.make_async_copy(adj_turbulence, first.at[4, 1 : nx + 1, body], load_sem.at[2]),
        pltpu.make_async_copy(adj_distance, first.at[5, 1 : nx + 1, body], load_sem.at[3]),
        pltpu.make_async_copy(velocity, flow.at[:, 1 : nx + 1, body], load_sem.at[4]),
        pltpu.make_async_copy(turbulence, turb, load_sem.at[5]),
        pltpu.make_async_copy(wall_distance, wall, load_sem.at[6]),
        pltpu.make_async_copy(porosity, poros, load_sem.at[7]),
        pltpu.make_async_copy(solid_mask, solid, load_sem.at[8]),
    ]
    for load in loads:
        load.start()

    barrier = pltpu.get_barrier_semaphore()
    others = []
    for k in range(1, group):
        flat = lax.rem(me + k, group)
        others.append({"gx": lax.div(flat, ngz), "gz": lax.rem(flat, ngz)})
    for other in others:
        pl.semaphore_signal(barrier, inc=1, device_id=other, device_id_type=MESH)
    pl.semaphore_wait(barrier, group - 1)

    def face(side, slot, source, target):
        step = -1 if side == 0 else 1
        return pltpu.make_async_remote_copy(
            src_ref=source,
            dst_ref=target,
            send_sem=face_send_sem.at[side, slot],
            recv_sem=face_recv_sem.at[side, slot],
            device_id={"gx": jnp.clip(gx + step, 0, ngx - 1)},
            device_id_type=MESH,
        )

    def faces_of(side):
        plane, halo = (0, nx + 1) if side == 0 else (nx - 1, 0)
        return [
            face(side, 0, adj_velocity.at[:, plane], first.at[0:3, halo, body]),
            face(side, 1, adj_pressure.at[plane], first.at[3, halo, body]),
            face(side, 2, adj_turbulence.at[plane], first.at[4, halo, body]),
            face(side, 3, adj_distance.at[plane], first.at[5, halo, body]),
            face(side, 4, velocity.at[:, plane], flow.at[:, halo, body]),
        ]

    def later_faces_of(side):
        plane, halo = (1, nx + 1) if side == 0 else (nx, 0)
        return [face(side, 5, second.at[:, plane, body], second.at[:, halo, body])]

    sends_to = (has_low, has_high)
    takes_from = (has_high, has_low)

    def start_faces(make):
        for side in (0, 1):
            @pl.when(sends_to[side])
            def _():
                for copy in make(side):
                    copy.start()

    def wait_faces(make):
        for side in (0, 1):
            @pl.when(takes_from[side])
            def _():
                for copy in make(side):
                    copy.wait_recv()

    def finish_faces(make):
        for side in (0, 1):
            @pl.when(sends_to[side])
            def _():
                for copy in make(side):
                    copy.wait_send()

    start_faces(faces_of)

    def clear(x, carry):
        blank = jnp.zeros((PAD, nz), jnp.float32)
        for f in range(6):
            for field in (first, second):
                field[f, x, 0:PAD] = blank
                field[f, x, PAD + ny : 2 * PAD + ny] = blank
        for f in range(3):
            flow[f, x, 0:PAD] = blank
            flow[f, x, PAD + ny : 2 * PAD + ny] = blank
        return carry

    lax.fori_loop(1, nx + 1, clear, 0)
    for missing, halo in ((gx == 0, 0), (gx == ngx - 1, nx + 1)):
        @pl.when(missing)
        def _():
            blank = jnp.zeros((ny, nz), jnp.float32)
            for f in range(6):
                first[f, halo, body] = blank
                second[f, halo, body] = blank
            for f in range(3):
                flow[f, halo, body] = blank

    lane = lax.broadcasted_iota(jnp.int32, (ROWS, nz), 1)
    edge = jnp.where(gz == 0, nz - 1, 0)
    at_edge = lane == edge
    at_first = lane == 0
    at_last = lane == nz - 1

    def pack(field, count, slot):
        def step(k, carry):
            r = pl.multiple_of(k * ROWS, ROWS)
            packed = jnp.zeros((ROWS, nz), jnp.float32)
            for f in range(count):
                for x in range(nx):
                    spot = f * nx + x
                    cells = field[f, x + 1, pl.ds(r + PAD, ROWS)]
                    shift = lax.rem(spot - edge + nz, nz)
                    packed = jnp.where(lane == spot, pltpu.roll(cells, shift, 1), packed)
            edge_send[slot, pl.ds(r, ROWS)] = packed
            return carry

        lax.fori_loop(0, chunks, step, 0)

    def edge_copy(slot):
        return pltpu.make_async_remote_copy(
            src_ref=edge_send.at[slot],
            dst_ref=edge_recv.at[slot],
            send_sem=edge_send_sem.at[slot],
            recv_sem=edge_recv_sem.at[slot],
            device_id={"gz": 1 - gz},
            device_id_type=MESH,
        )

    for load in loads[:4]:
        load.wait()
    pack(first, 6, 0)
    edge_copy(0).start()
    loads[4].wait()
    pack(flow, 3, 1)
    edge_copy(1).start()
    for load in loads[5:]:
        load.wait()
    edge_copy(0).wait_recv()
    edge_copy(1).wait_recv()

    def neighbours(field, f, x, r, packed):
        centre = field[f, x + 1, pl.ds(r + PAD, ROWS)]
        x_plus = field[f, x + 2, pl.ds(r + PAD, ROWS)]
        x_minus = field[f, x, pl.ds(r + PAD, ROWS)]
        y_plus = field[f, x + 1, pl.ds(r + PAD + 1, ROWS)]
        y_minus = field[f, x + 1, pl.ds(r + PAD - 1, ROWS)]
        shift = lax.rem(edge - (f * nx + x) + nz, nz)
        outside = jnp.where(at_edge, pltpu.roll(packed, shift, 1), 0.0)
        z_plus = jnp.where(at_last, outside, pltpu.roll(centre, nz - 1, 1))
        z_minus = jnp.where(at_first, outside, pltpu.roll(centre, 1, 1))
        return centre, x_plus, x_minus, y_plus, y_minus, z_plus, z_minus

    def cell_block(source, slot, is_last, x, k, carry):
        r = pl.multiple_of(k * ROWS, ROWS)
        rows = pl.ds(r, ROWS)
        packed = edge_recv[slot, rows]
        vel = [flow[c, x + 1, pl.ds(r + PAD, ROWS)] for c in range(3)]
        tur = turb[x, rows]
        por = poros[x, rows]
        viscous = VISCOSITY + tur
        if is_last:
            inv_flow = coefs[0, x, rows]
            inv_turb = coefs[1, x, rows]
            coupled = coefs[2, x, rows]
            shear = coefs[3, x, rows]
        else:
            sol = solid[x, rows].astype(jnp.float32)
            inv_wall = 1.0 / wall[x, rows]
            inv_wall2 = inv_wall * inv_wall
            inv_flow = 1.0 / (6.0 * viscous + por + PENALTY * sol)
            inv_turb = 1.0 / (6.0 * viscous + (DESTRUCTION * tur) * inv_wall2)
            coupled = (2.0 * DESTRUCTION * tur) * tur * (inv_wall2 * inv_wall)
            packed_flow = edge_recv[1, rows]
            square = jnp.zeros((ROWS, nz), jnp.float32)
            for c in range(3):
                _, xp, xm, yp, ym, zp, zm = neighbours(flow, c, x, r, packed_flow)
                dx, dy, dz = xp - xm, yp - ym, zp - zm
                square = square + (dx * dx + dy * dy + dz * dz)
            shear = square * (0.25 * COUPLING / 9.0)
            coefs[0, x, rows] = inv_flow
            coefs[1, x, rows] = inv_turb
            coefs[2, x, rows] = coupled
            coefs[3, x, rows] = shear

        near = [neighbours(source, f, x, r, packed) for f in range(6)]
        half = [0.5 * v for v in vel]
        plus = [viscous + h for h in half]
        minus = [viscous - h for h in half]

        def moved(f):
            _, xp, xm, yp, ym, zp, zm = near[f]
            return (
                (plus[0] * xp + minus[0] * xm)
                + (plus[1] * yp + minus[1] * ym)
                + (plus[2] * zp + minus[2] * zm)
            )

        def laplace(f):
            _, xp, xm, yp, ym, zp, zm = near[f]
            return (xp + xm) + (yp + ym) + (zp + zm)

        def rise(f, axis):
            return near[f][1 + 2 * axis] - near[f][2 + 2 * axis]

        old = [n[0] for n in near]
        drive = por + COUPLING * old[4]
        new = [
            (moved(c) + (vel[c] * drive - 0.5 * rise(3, c))) * inv_flow for c in range(3)
        ]
        split = rise(0, 0) + rise(1, 1) + rise(2, 2)
        new.append((laplace(3) - 0.5 * split) * (1.0 / 6.0))
        work = vel[0] * old[0] + vel[1] * old[1] + vel[2] * old[2]
        new.append((moved(4) + (shear + COUPLING * work)) * inv_turb)
        new.append((laplace(5) + coupled * old[4]) * (1.0 / (6.0 + DISTANCE_DAMPING)))
        if is_last:
            for c in range(3):
                new_velocity[c, x, rows] = new[c]
            new_pressure[x, rows] = new[3]
            new_turbulence[x, rows] = new[4]
            new_distance[x, rows] = new[5]
            sol = solid[x, rows].astype(jnp.float32)
            sensitivity[x, rows] = (1.0 - sol) * (
                vel[0] * new[0] + vel[1] * new[1] + vel[2] * new[2]
            )
        else:
            for f in range(6):
                second[f, x + 1, pl.ds(r + PAD, ROWS)] = new[f]
        delta = [(new[f] - old[f]) for f in range(6)]
        square = [d * d for d in delta]
        return (
            carry[0] + (square[0] + square[1] + square[2]),
            carry[1] + square[3],
            carry[2] + square[4],
            carry[3] + square[5],
        )

    def planes(source, slot, is_last, count, place, carry):
        def step(i, carry):
            x = place(lax.div(i, chunks))
            return cell_block(source, slot, is_last, x, lax.rem(i, chunks), carry)

        return lax.fori_loop(0, count * chunks, step, carry, unroll=2)

    def inner(i):
        return i + 1

    def outer(i):
        return i * (nx - 1)

    zero = tuple(jnp.zeros((ROWS, nz), jnp.float32) for _ in range(4))

    totals = planes(first, 0, False, nx - 2, inner, zero)
    wait_faces(faces_of)
    totals = planes(first, 0, False, 2, outer, totals)
    start_faces(later_faces_of)
    for j in range(4):
        sums[pl.ds(j, 1)] = jnp.sum(totals[j], axis=0, keepdims=True)

    pack(second, 6, 2)
    edge_copy(2).start()
    edge_copy(2).wait_recv()
    totals = planes(second, 2, True, nx - 2, inner, zero)
    wait_faces(later_faces_of)
    totals = planes(second, 2, True, 2, outer, totals)
    for j in range(4):
        sums[pl.ds(4 + j, 1)] = jnp.sum(totals[j], axis=0, keepdims=True)

    def sum_copy(k):
        return pltpu.make_async_remote_copy(
            src_ref=sums,
            dst_ref=all_sums.at[k],
            send_sem=sum_send_sem.at[k],
            recv_sem=sum_recv_sem.at[k],
            device_id=others[k],
            device_id_type=MESH,
        )

    for k in range(group - 1):
        sum_copy(k).start()
    finish_faces(faces_of)
    finish_faces(later_faces_of)
    for slot in range(3):
        edge_copy(slot).wait_send()
    whole = sums[...]
    for k in range(group - 1):
        sum_copy(k).wait_recv()
        whole = whole + all_sums[k]
    for k in range(group - 1):
        sum_copy(k).wait_send()
    total = jnp.sum(whole, axis=1, keepdims=True)
    root = jnp.broadcast_to(jnp.sqrt(total + 1e-06), (8, nz))
    norms[...] = root


def local(mesh_shape, *args):
    ngx, ngz = mesh_shape
    assert ngz == 2
    nx, ny, nz = args[1].shape
    assert 6 * nx <= nz and ny % ROWS == 0
    f32 = jnp.float32
    cells = jax.ShapeDtypeStruct((nx, ny, nz), f32)
    group = ngx * ngz
    tall = (nx + 2, ny + 2 * PAD, nz)
    outs = pl.pallas_call(
        functools.partial(kernel, ngx, ngz),
        out_shape=[
            jax.ShapeDtypeStruct((3, nx, ny, nz), f32),
            cells,
            cells,
            cells,
            cells,
            jax.ShapeDtypeStruct((8, nz), f32),
        ],
        in_specs=[pl.BlockSpec(memory_space=pl.ANY)] * 9,
        out_specs=[pl.BlockSpec(memory_space=pltpu.VMEM)] * 6,
        scratch_shapes=[
            pltpu.VMEM((6,) + tall, f32),
            pltpu.VMEM((6,) + tall, f32),
            pltpu.VMEM((3,) + tall, f32),
            pltpu.VMEM((nx, ny, nz), f32),
            pltpu.VMEM((nx, ny, nz), f32),
            pltpu.VMEM((nx, ny, nz), f32),
            pltpu.VMEM((nx, ny, nz), jnp.int32),
            pltpu.VMEM((4, nx, ny, nz), f32),
            pltpu.VMEM((3, ny, nz), f32),
            pltpu.VMEM((3, ny, nz), f32),
            pltpu.VMEM((8, nz), f32),
            pltpu.VMEM((group - 1, 8, nz), f32),
            pltpu.SemaphoreType.DMA((9,)),
            pltpu.SemaphoreType.DMA((2, 6)),
            pltpu.SemaphoreType.DMA((2, 6)),
            pltpu.SemaphoreType.DMA((3,)),
            pltpu.SemaphoreType.DMA((3,)),
            pltpu.SemaphoreType.DMA((group - 1,)),
            pltpu.SemaphoreType.DMA((group - 1,)),
        ],
        compiler_params=pltpu.CompilerParams(
            collective_id=0,
            has_side_effects=True,
            vmem_limit_bytes=52 * 1024 * 1024,
        ),
    )(*args)
    return (*outs[:5], outs[5][:, 0])


def solution(mesh):
    cells = P("gx", "parts", "gz")
    vector = P(None, "gx", "parts", "gz")
    in_specs = (vector, cells, cells, cells, cells, vector, cells, cells, cells)
    out_specs = (vector, cells, cells, cells, cells, P("parts"))
    return jax.shard_map(
        functools.partial(local, (mesh.shape["gx"], mesh.shape["gz"])),
        mesh=mesh,
        in_specs=in_specs,
        out_specs=out_specs,
        check_vma=False,
    )
```

profile of v0, /device:TPU:0, one launch (start us, length us, event | category | flops | bytes accessed | tf_op | source)
XLA Modules:
  0.0 71.6 jit_solution(17460648369986210565)
XLA Ops:
  0.6 62.5 %shard_map.136 = (f32[3,16,128,128]{3,2,1,0:T(8,128)}, f32[16,128,128]{2,1,0:T(8,128)S(1)}, f32[16,128,128]{2,1,0:T(8,128)}, f32[16,128,128]{2,1,0:T(8,128)}, f3...) custom-call(f32[3,16,128,128]{3,2,1,0:T(8,128)} %velocity.1, f32[16,128,128]{2,1,0:T(8,128)} %turbulence.1, ...), custom_call_target="tpu_custom_call" | custom-call | tf_op jit(solution)/shard_map/pallas_call | solution.py:370
  63.1 0.6 slice_reduce_fusion
  63.7 0.0 copy-start.2
  63.7 4.0 %copy.20 = f32[3,16,128,128]{3,2,1,0:T(8,128)} copy(f32[3,16,128,128]{3,2,1,0:T(8,128)} %get-tuple-element.24) | data formatting | bytes 6291456
  67.7 0.0 copy-start.1
  67.7 0.0 copy-start
  67.7 1.0 %copy.21 = f32[16,128,128]{2,1,0:T(8,128)} copy(f32[16,128,128]{2,1,0:T(8,128)S(1)} %get-tuple-element.25) | data formatting | bytes 2097152
  68.7 0.0 copy-done.2
  68.7 1.0 %copy.22 = f32[16,128,128]{2,1,0:T(8,128)} copy(f32[16,128,128]{2,1,0:T(8,128)S(1)} %copy-done.2) | data formatting | bytes 2097152
  69.7 0.0 copy-done.1
  69.7 1.0 %copy.23 = f32[16,128,128]{2,1,0:T(8,128)} copy(f32[16,128,128]{2,1,0:T(8,128)S(1)} %copy-done.1) | data formatting | bytes 2097152
  70.6 0.0 copy-done
  70.7 1.0 %copy.24 = f32[16,128,128]{2,1,0:T(8,128)} copy(f32[16,128,128]{2,1,0:T(8,128)S(1)} %copy-done) | data formatting | bytes 2097152
Async XLA Ops:
  63.7 5.0 %copy-start.2 = (f32[16,128,128]{2,1,0:T(8,128)S(1)}, f32[16,128,128]{2,1,0:T(8,128)}, u32[]{:S(2)}) copy-start(f32[16,128,128]{2,1,0:T(8,128)} %get-tuple-element.26) | copy-start | bytes 3145732
  67.7 1.9 %copy-start.1 = (f32[16,128,128]{2,1,0:T(8,128)S(1)}, f32[16,128,128]{2,1,0:T(8,128)}, u32[]{:S(2)}) copy-start(f32[16,128,128]{2,1,0:T(8,128)} %get-tuple-element.27) | copy-start | bytes 3145732
  67.7 2.9 %copy-start = (f32[16,128,128]{2,1,0:T(8,128)S(1)}, f32[16,128,128]{2,1,0:T(8,128)}, u32[]{:S(2)}) copy-start(f32[16,128,128]{2,1,0:T(8,128)} %get-tuple-element.28) | copy-start | bytes 3145732
where the time goes:
time: 71.8 us; the launch traced here: 71.6 us
  Pallas kernels  62.5 us (87%)
  local copies, waits for them, and re-layouts  8.51 us (12%)
    pallas_call x1, Pallas kernels, local(): pl.pallas_call(functools.partial(kernel, ngx, ngz), out_shape=[jax.ShapeD...  62.5 us
    unnamed x11, local copies, waits for them, and re-layouts  7.89 us

commit v1 on v0

--- a/solution.py
+++ b/solution.py
@@ -13,7 +13,7 @@
 DISTANCE_DAMPING = 0.5
 PENALTY = 20.0
 PAD = 8
-ROWS = 8
+ROWS = 16
 MESH = pl.DeviceIdType.MESH
 
 
@@ -47,6 +47,12 @@
     edge_recv,
     sums,
     all_sums,
+    held_new_velocity,
+    held_new_pressure,
+    held_new_turbulence,
+    held_new_distance,
+    held_sensitivity,
+    store_sem,
     load_sem,
     face_send_sem,
     face_recv_sem,
@@ -76,9 +82,6 @@
         pltpu.make_async_copy(porosity, poros, load_sem.at[7]),
         pltpu.make_async_copy(solid_mask, solid, load_sem.at[8]),
     ]
-    for load in loads:
-        load.start()
-
     barrier = pltpu.get_barrier_semaphore()
     others = []
     for k in range(1, group):
@@ -106,12 +109,22 @@
             face(side, 1, adj_pressure.at[plane], first.at[3, halo, body]),
             face(side, 2, adj_turbulence.at[plane], first.at[4, halo, body]),
             face(side, 3, adj_distance.at[plane], first.at[5, halo, body]),
-            face(side, 4, velocity.at[:, plane], flow.at[:, halo, body]),
         ]
+
+    def flow_faces_of(side):
+        plane, halo = (0, nx + 1) if side == 0 else (nx - 1, 0)
+        return [face(side, 4, velocity.at[:, plane], flow.at[:, halo, body])]
 
     def later_faces_of(side):
         plane, halo = (1, nx + 1) if side == 0 else (nx, 0)
-        return [face(side, 5, second.at[:, plane, body], second.at[:, halo, body])]
+        return [
+            face(side, 5, second.at[0:4, plane, body], second.at[0:4, halo, body]),
+            face(side, 6, second.at[5, plane, body], second.at[5, halo, body]),
+        ]
+
+    def later_turb_of(side):
+        plane, halo = (1, nx + 1) if side == 0 else (nx, 0)
+        return [face(side, 7, second.at[4, plane, body], second.at[4, halo, body])]
 
     sends_to = (has_low, has_high)
     takes_from = (has_high, has_low)
@@ -138,6 +151,9 @@
                     copy.wait_send()
 
     start_faces(faces_of)
+    start_faces(flow_faces_of)
+    for load in loads:
+        load.start()
 
     def clear(x, carry):
         blank = jnp.zeros((PAD, nz), jnp.float32)
@@ -216,96 +232,111 @@
         z_minus = jnp.where(at_first, outside, pltpu.roll(centre, 1, 1))
         return centre, x_plus, x_minus, y_plus, y_minus, z_plus, z_minus
 
-    def cell_block(source, slot, is_last, x, k, carry):
+    def cell_block(source, slot, is_last, groups, x, k, carry):
         r = pl.multiple_of(k * ROWS, ROWS)
         rows = pl.ds(r, ROWS)
+        tall_rows = pl.ds(r + PAD, ROWS)
         packed = edge_recv[slot, rows]
-        vel = [flow[c, x + 1, pl.ds(r + PAD, ROWS)] for c in range(3)]
+        vel = [flow[c, x + 1, tall_rows] for c in range(3)]
         tur = turb[x, rows]
-        por = poros[x, rows]
         viscous = VISCOSITY + tur
-        if is_last:
-            inv_flow = coefs[0, x, rows]
-            inv_turb = coefs[1, x, rows]
-            coupled = coefs[2, x, rows]
-            shear = coefs[3, x, rows]
-        else:
-            sol = solid[x, rows].astype(jnp.float32)
-            inv_wall = 1.0 / wall[x, rows]
-            inv_wall2 = inv_wall * inv_wall
-            inv_flow = 1.0 / (6.0 * viscous + por + PENALTY * sol)
-            inv_turb = 1.0 / (6.0 * viscous + (DESTRUCTION * tur) * inv_wall2)
-            coupled = (2.0 * DESTRUCTION * tur) * tur * (inv_wall2 * inv_wall)
-            packed_flow = edge_recv[1, rows]
-            square = jnp.zeros((ROWS, nz), jnp.float32)
-            for c in range(3):
-                _, xp, xm, yp, ym, zp, zm = neighbours(flow, c, x, r, packed_flow)
-                dx, dy, dz = xp - xm, yp - ym, zp - zm
-                square = square + (dx * dx + dy * dy + dz * dz)
-            shear = square * (0.25 * COUPLING / 9.0)
-            coefs[0, x, rows] = inv_flow
-            coefs[1, x, rows] = inv_turb
-            coefs[2, x, rows] = coupled
-            coefs[3, x, rows] = shear
-
-        near = [neighbours(source, f, x, r, packed) for f in range(6)]
         half = [0.5 * v for v in vel]
         plus = [viscous + h for h in half]
         minus = [viscous - h for h in half]
-
-        def moved(f):
-            _, xp, xm, yp, ym, zp, zm = near[f]
+        old_turb = source[4, x + 1, tall_rows]
+        old = {}
+        new = {}
+
+        def near_of(f):
+            centre, *sides = neighbours(source, f, x, r, packed)
+            old[f] = centre
+            return sides
+
+        def moved(sides):
+            xp, xm, yp, ym, zp, zm = sides
             return (
                 (plus[0] * xp + minus[0] * xm)
                 + (plus[1] * yp + minus[1] * ym)
                 + (plus[2] * zp + minus[2] * zm)
             )
 
-        def laplace(f):
-            _, xp, xm, yp, ym, zp, zm = near[f]
+        def laplace(sides):
+            xp, xm, yp, ym, zp, zm = sides
             return (xp + xm) + (yp + ym) + (zp + zm)
 
-        def rise(f, axis):
-            return near[f][1 + 2 * axis] - near[f][2 + 2 * axis]
-
-        old = [n[0] for n in near]
-        drive = por + COUPLING * old[4]
-        new = [
-            (moved(c) + (vel[c] * drive - 0.5 * rise(3, c))) * inv_flow for c in range(3)
-        ]
-        split = rise(0, 0) + rise(1, 1) + rise(2, 2)
-        new.append((laplace(3) - 0.5 * split) * (1.0 / 6.0))
-        work = vel[0] * old[0] + vel[1] * old[1] + vel[2] * old[2]
-        new.append((moved(4) + (shear + COUPLING * work)) * inv_turb)
-        new.append((laplace(5) + coupled * old[4]) * (1.0 / (6.0 + DISTANCE_DAMPING)))
+        if "rest" in groups:
+            por = poros[x, rows]
+            if is_last:
+                inv_flow = coefs[0, x, rows]
+                coupled = coefs[2, x, rows]
+            else:
+                sol = solid[x, rows].astype(jnp.float32)
+                inv_wall = 1.0 / wall[x, rows]
+                inv_wall2 = inv_wall * inv_wall
+                inv_flow = 1.0 / (6.0 * viscous + por + PENALTY * sol)
+                inv_turb = 1.0 / (6.0 * viscous + (DESTRUCTION * tur) * inv_wall2)
+                coupled = (2.0 * DESTRUCTION * tur) * tur * (inv_wall2 * inv_wall)
+                coefs[0, x, rows] = inv_flow
+                coefs[1, x, rows] = inv_turb
+                coefs[2, x, rows] = coupled
+            drive = por + COUPLING * old_turb
+            press = near_of(3)
+            split = None
+            for c in range(3):
+                sides = near_of(c)
+                push = 0.5 * (press[2 * c] - press[2 * c + 1])
+                new[c] = (moved(sides) + (vel[c] * drive - push)) * inv_flow
+                rise = sides[2 * c] - sides[2 * c + 1]
+                split = rise if split is None else split + rise
+            new[3] = (laplace(press) - 0.5 * split) * (1.0 / 6.0)
+            new[5] = (laplace(near_of(5)) + coupled * old_turb) * (
+                1.0 / (6.0 + DISTANCE_DAMPING)
+            )
+        if "turb" in groups:
+            if is_last:
+                shear = coefs[3, x, rows]
+            else:
+                packed_flow = edge_recv[1, rows]
+                square = jnp.zeros((ROWS, nz), jnp.float32)
+                for c in range(3):
+                    _, xp, xm, yp, ym, zp, zm = neighbours(flow, c, x, r, packed_flow)
+                    dx, dy, dz = xp - xm, yp - ym, zp - zm
+                    square = square + (dx * dx + dy * dy + dz * dz)
+                shear = square * (0.25 * COUPLING / 9.0)
+                coefs[3, x, rows] = shear
+            if is_last or "rest" not in groups:
+                inv_turb = coefs[1, x, rows]
+            u = [source[c, x + 1, tall_rows] for c in range(3)]
+            work = vel[0] * u[0] + vel[1] * u[1] + vel[2] * u[2]
+            new[4] = (moved(near_of(4)) + (shear + COUPLING * work)) * inv_turb
         if is_last:
             for c in range(3):
-                new_velocity[c, x, rows] = new[c]
-            new_pressure[x, rows] = new[3]
-            new_turbulence[x, rows] = new[4]
-            new_distance[x, rows] = new[5]
+                held_new_velocity[c, x, rows] = new[c]
+            held_new_pressure[x, rows] = new[3]
+            held_new_turbulence[x, rows] = new[4]
+            held_new_distance[x, rows] = new[5]
             sol = solid[x, rows].astype(jnp.float32)
-            sensitivity[x, rows] = (1.0 - sol) * (
+            held_sensitivity[x, rows] = (1.0 - sol) * (
                 vel[0] * new[0] + vel[1] * new[1] + vel[2] * new[2]
             )
         else:
-            for f in range(6):
-                second[f, x + 1, pl.ds(r + PAD, ROWS)] = new[f]
-        delta = [(new[f] - old[f]) for f in range(6)]
-        square = [d * d for d in delta]
-        return (
-            carry[0] + (square[0] + square[1] + square[2]),
-            carry[1] + square[3],
-            carry[2] + square[4],
-            carry[3] + square[5],
-        )
-
-    def planes(source, slot, is_last, count, place, carry):
+            for f in new:
+                second[f, x + 1, tall_rows] = new[f]
+        totals = list(carry)
+        for f in new:
+            delta = new[f] - old[f]
+            j = max(f - 2, 0)
+            totals[j] = totals[j] + delta * delta
+        return tuple(totals)
+
+    def planes(source, slot, is_last, count, place, carry, groups=("rest", "turb")):
         def step(i, carry):
             x = place(lax.div(i, chunks))
-            return cell_block(source, slot, is_last, x, lax.rem(i, chunks), carry)
-
-        return lax.fori_loop(0, count * chunks, step, carry, unroll=2)
+            return cell_block(
+                source, slot, is_last, groups, x, lax.rem(i, chunks), carry
+            )
+
+        return lax.fori_loop(0, count * chunks, step, carry, unroll=4)
 
     def inner(i):
         return i + 1
@@ -313,12 +344,39 @@
     def outer(i):
         return i * (nx - 1)
 
+    def stores(slot, span):
+        pairs = (
+            (held_new_pressure, new_pressure),
+            (held_new_turbulence, new_turbulence),
+            (held_new_distance, new_distance),
+            (held_sensitivity, sensitivity),
+        )
+        copies = [
+            pltpu.make_async_copy(
+                held_new_velocity.at[:, span], new_velocity.at[:, span], store_sem.at[slot, 4]
+            )
+        ]
+        for i, (held, out) in enumerate(pairs):
+            copies.append(
+                pltpu.make_async_copy(held.at[span], out.at[span], store_sem.at[slot, i])
+            )
+        return copies
+
+    all_stores = (
+        stores(0, pl.ds(1, nx - 2))
+        + stores(1, pl.ds(0, 1))
+        + stores(2, pl.ds(nx - 1, 1))
+    )
+
     zero = tuple(jnp.zeros((ROWS, nz), jnp.float32) for _ in range(4))
 
     totals = planes(first, 0, False, nx - 2, inner, zero)
     wait_faces(faces_of)
-    totals = planes(first, 0, False, 2, outer, totals)
+    totals = planes(first, 0, False, 2, outer, totals, ("rest",))
     start_faces(later_faces_of)
+    wait_faces(flow_faces_of)
+    totals = planes(first, 0, False, 2, outer, totals, ("turb",))
+    start_faces(later_turb_of)
     for j in range(4):
         sums[pl.ds(j, 1)] = jnp.sum(totals[j], axis=0, keepdims=True)
 
@@ -326,10 +384,16 @@
     edge_copy(2).start()
     edge_copy(2).wait_recv()
     totals = planes(second, 2, True, nx - 2, inner, zero)
+    for store in all_stores[:5]:
+        store.start()
     wait_faces(later_faces_of)
+    wait_faces(later_turb_of)
     totals = planes(second, 2, True, 2, outer, totals)
     for j in range(4):
         sums[pl.ds(4 + j, 1)] = jnp.sum(totals[j], axis=0, keepdims=True)
+
+    for store in all_stores[5:]:
+        store.start()
 
     def sum_copy(k):
         return pltpu.make_async_remote_copy(
@@ -344,7 +408,9 @@
     for k in range(group - 1):
         sum_copy(k).start()
     finish_faces(faces_of)
+    finish_faces(flow_faces_of)
     finish_faces(later_faces_of)
+    finish_faces(later_turb_of)
     for slot in range(3):
         edge_copy(slot).wait_send()
     whole = sums[...]
@@ -353,6 +419,8 @@
         whole = whole + all_sums[k]
     for k in range(group - 1):
         sum_copy(k).wait_send()
+    for store in all_stores:
+        store.wait()
     total = jnp.sum(whole, axis=1, keepdims=True)
     root = jnp.broadcast_to(jnp.sqrt(total + 1e-06), (8, nz))
     norms[...] = root
@@ -378,7 +446,8 @@
             jax.ShapeDtypeStruct((8, nz), f32),
         ],
         in_specs=[pl.BlockSpec(memory_space=pl.ANY)] * 9,
-        out_specs=[pl.BlockSpec(memory_space=pltpu.VMEM)] * 6,
+        out_specs=[pl.BlockSpec(memory_space=pl.ANY)] * 5
+        + [pl.BlockSpec(memory_space=pltpu.VMEM)],
         scratch_shapes=[
             pltpu.VMEM((6,) + tall, f32),
             pltpu.VMEM((6,) + tall, f32),
@@ -392,9 +461,15 @@
             pltpu.VMEM((3, ny, nz), f32),
             pltpu.VMEM((8, nz), f32),
             pltpu.VMEM((group - 1, 8, nz), f32),
+            pltpu.VMEM((3, nx, ny, nz), f32),
+            pltpu.VMEM((nx, ny, nz), f32),
+            pltpu.VMEM((nx, ny, nz), f32),
+            pltpu.VMEM((nx, ny, nz), f32),
+            pltpu.VMEM((nx, ny, nz), f32),
+            pltpu.SemaphoreType.DMA((3, 5)),
             pltpu.SemaphoreType.DMA((9,)),
-            pltpu.SemaphoreType.DMA((2, 6)),
-            pltpu.SemaphoreType.DMA((2, 6)),
+            pltpu.SemaphoreType.DMA((2, 8)),
+            pltpu.SemaphoreType.DMA((2, 8)),
             pltpu.SemaphoreType.DMA((3,)),
             pltpu.SemaphoreType.DMA((3,)),
             pltpu.SemaphoreType.DMA((group - 1,)),

time: 71.8 us -> 66.9 us (0.932)
  Pallas kernels: 62.5 us -> 57.6 us
    pallas_call x1, Pallas kernels: 62.5 us -> 57.6 us  [local(): pl.pallas_call(functools.partial(kernel, ngx, ngz), out_shape=[jax.ShapeD...]
where the time goes in v1:
time: 66.9 us; the launch traced here: 66.7 us
  Pallas kernels  57.6 us (86%)
  local copies, waits for them, and re-layouts  8.51 us (13%)
    pallas_call x1, Pallas kernels, local(): pl.pallas_call(functools.partial(kernel, ngx, ngz), out_shape=[jax.ShapeD...  57.6 us
    unnamed x11, local copies, waits for them, and re-layouts  7.89 us

profile of v1, /device:TPU:0, one launch (start us, length us, event | category | flops | bytes accessed | tf_op | source)
XLA Modules:
  0.0 66.7 jit_solution(14985057698459596245)
XLA Ops:
  0.6 57.6 %shard_map.136 = (f32[3,16,128,128]{3,2,1,0:T(8,128)}, f32[16,128,128]{2,1,0:T(8,128)S(1)}, f32[16,128,128]{2,1,0:T(8,128)}, f32[16,128,128]{2,1,0:T(8,128)}, f3...) custom-call(f32[3,16,128,128]{3,2,1,0:T(8,128)} %velocity.1, f32[16,128,128]{2,1,0:T(8,128)} %turbulence.1, ...), custom_call_target="tpu_custom_call" | custom-call | tf_op jit(solution)/shard_map/pallas_call | solution.py:438
  58.2 0.6 slice_reduce_fusion
  58.8 0.0 copy-start.2
  58.8 4.0 %copy.20 = f32[3,16,128,128]{3,2,1,0:T(8,128)} copy(f32[3,16,128,128]{3,2,1,0:T(8,128)} %get-tuple-element.24) | data formatting | bytes 6291456
  62.8 0.0 copy-start.1
  62.8 0.0 copy-start
  62.8 1.0 %copy.21 = f32[16,128,128]{2,1,0:T(8,128)} copy(f32[16,128,128]{2,1,0:T(8,128)S(1)} %get-tuple-element.25) | data formatting | bytes 2097152
  63.8 0.0 copy-done.2
  63.8 1.0 %copy.22 = f32[16,128,128]{2,1,0:T(8,128)} copy(f32[16,128,128]{2,1,0:T(8,128)S(1)} %copy-done.2) | data formatting | bytes 2097152
  64.8 0.0 copy-done.1
  64.8 1.0 %copy.23 = f32[16,128,128]{2,1,0:T(8,128)} copy(f32[16,128,128]{2,1,0:T(8,128)S(1)} %copy-done.1) | data formatting | bytes 2097152
  65.8 0.0 copy-done
  65.8 1.0 %copy.24 = f32[16,128,128]{2,1,0:T(8,128)} copy(f32[16,128,128]{2,1,0:T(8,128)S(1)} %copy-done) | data formatting | bytes 2097152
Async XLA Ops:
  58.8 5.0 %copy-start.2 = (f32[16,128,128]{2,1,0:T(8,128)S(1)}, f32[16,128,128]{2,1,0:T(8,128)}, u32[]{:S(2)}) copy-start(f32[16,128,128]{2,1,0:T(8,128)} %get-tuple-element.26) | copy-start | bytes 3145732
  62.8 1.9 %copy-start.1 = (f32[16,128,128]{2,1,0:T(8,128)S(1)}, f32[16,128,128]{2,1,0:T(8,128)}, u32[]{:S(2)}) copy-start(f32[16,128,128]{2,1,0:T(8,128)} %get-tuple-element.27) | copy-start | bytes 3145732
  62.8 2.9 %copy-start = (f32[16,128,128]{2,1,0:T(8,128)S(1)}, f32[16,128,128]{2,1,0:T(8,128)}, u32[]{:S(2)}) copy-start(f32[16,128,128]{2,1,0:T(8,128)} %get-tuple-element.28) | copy-start | bytes 3145732

commit v2 on v1

--- a/solution.py
+++ b/solution.py
@@ -426,6 +426,11 @@
     norms[...] = root
 
 
+def hand_over(*refs):
+    for i in range(5):
+        refs[5 + i][...] = refs[i][...]
+
+
 def local(mesh_shape, *args):
     ngx, ngz = mesh_shape
     assert ngz == 2
@@ -481,7 +486,18 @@
             vmem_limit_bytes=52 * 1024 * 1024,
         ),
     )(*args)
-    return (*outs[:5], outs[5][:, 0])
+    step = 4
+    flat = pl.BlockSpec((step, ny, nz), lambda i: (i, 0, 0))
+    tall_block = pl.BlockSpec((3, step, ny, nz), lambda i: (0, i, 0, 0))
+    fields = pl.pallas_call(
+        hand_over,
+        grid=(nx // step,),
+        out_shape=[jax.ShapeDtypeStruct(o.shape, o.dtype) for o in outs[:5]],
+        in_specs=[tall_block] + [flat] * 4,
+        out_specs=[tall_block] + [flat] * 4,
+        compiler_params=pltpu.CompilerParams(vmem_limit_bytes=52 * 1024 * 1024),
+    )(*outs[:5])
+    return (*fields, outs[5][:, 0])
 
 
 def solution(mesh):

time: 66.9 us -> 65.1 us (0.973)
  local copies, waits for them, and re-layouts: 8.51 us -> 0.62 us
  Pallas kernels: 57.6 us -> 63.6 us
    unnamed x11 -> x0, local copies, waits for them, and re-layouts: 7.89 us -> none
    pallas_call x0 -> x1, Pallas kernels: none -> 6.06 us  [local(): pl.pallas_call(hand_over, grid=(nx // step,), out_shape=[jax.ShapeDtypeSt...]
where the time goes in v2:
time: 65.1 us; the launch traced here: 64.9 us
  Pallas kernels  63.6 us (98%)
    pallas_call x1, Pallas kernels, local(): pl.pallas_call(functools.partial(kernel, ngx, ngz), out_shape=[jax.ShapeD...  57.6 us
    pallas_call x1, Pallas kernels, local(): pl.pallas_call(hand_over, grid=(nx // step,), out_shape=[jax.ShapeDtypeSt...  6.06 us

profile of v2, /device:TPU:0, one launch (start us, length us, event | category | flops | bytes accessed | tf_op | source)
XLA Modules:
  0.0 64.9 jit_solution(7302357510879495889)
XLA Ops:
  0.6 57.6 %shard_map.136 = (f32[3,16,128,128]{3,2,1,0:T(8,128)}, f32[16,128,128]{2,1,0:T(8,128)S(1)}, f32[16,128,128]{2,1,0:T(8,128)}, f32[16,128,128]{2,1,0:T(8,128)}, f3...) custom-call(f32[3,16,128,128]{3,2,1,0:T(8,128)} %velocity.1, f32[16,128,128]{2,1,0:T(8,128)} %turbulence.1, ...), custom_call_target="tpu_custom_call" | custom-call | tf_op jit(solution)/shard_map/pallas_call | solution.py:443
  58.2 6.1 %shard_map.137 = (f32[3,16,128,128]{3,2,1,0:T(8,128)}, f32[16,128,128]{2,1,0:T(8,128)}, f32[16,128,128]{2,1,0:T(8,128)}, f32[16,128,128]{2,1,0:T(8,128)}, f32[16,128,128]{2,1,0:T(8,128)}) custom-call(f32[3,16,128,128]{3,2,1,0:T(8,128)} %get-tuple-element.17.refs_0_, f32[16,128,128]{2,1,0:T(8,128)S(1)} %get-tuple-element.18.refs_1_, ...), custom_call_target="tpu_custom_call" | custom-call | tf_op jit(solution)/shard_map/pallas_call | solution.py:492
  64.3 0.6 slice_reduce_fusion
